TPU v7x, 32 devices: a whole 2x2x4 slice. The times are simulated.
32 devices in a mesh: section: 8 (over y, x, core), batch: 4 (over z).
Axes of the slice: x: 2, y: 2, z: 4, core: 2. Of those that a mesh axis runs over, the one named last changes fastest.
Arguments:
- states: bfloat16 [16, 8, 64, 1024], P('section', 'batch'), may hold values from -6 to 6
- weights: bfloat16 [16, 64, 576], P('section'), may hold values from -0.25 to 0.25
- guess: float32 [8, 8, 64, 1024], P('section', 'batch'), may hold values from -6 to 6
- loss_cotangent: float32 [8, 64, 1024], P('batch'), may hold values from -6 to 6
Outputs:
- start_cotangents: float32 [8, 8, 64, 1024], P('section', 'batch')
- weight_grads: float32 [16, 36864], P('section', 'batch')
All inputs are finite; a program needn't handle non-finite values.
Results may differ from a plain program's by a relative error of at most 0.0039.
Values may be sent and summed in bfloat16 or wider, within the bound.
A program may use at most 128 MiB of HBM per device.

v0:
```python
import math

import jax
import jax.numpy as jnp
from jax import lax
from jax.sharding import PartitionSpec as P

STEP = 0.0625


def passed_along(block, axis, distance):
    devices = range(lax.axis_size(axis))
    route = [(i - distance, i) for i in devices if i - distance in devices]
    return lax.ppermute(block, axis, route)


def unfold_taps(values, pixel_side, direction):
    length = values.shape[-1]
    margin = pixel_side + 1
    widths = [(0, 0)] * (values.ndim - 1) + [(margin, margin)]
    padded = jnp.pad(values, widths)
    column_base = jnp.arange(length) % pixel_side
    copies = []
    for row_step in (-1, 0, 1):
        for col_step in (-1, 0, 1):
            delta = direction * (row_step * pixel_side + col_step)
            window = lax.slice_in_dim(
                padded, margin + delta, margin + delta + length, axis=values.ndim - 1
            )
            column = column_base + direction * col_step
            inside = (column >= 0) & (column < pixel_side)
            copies.append(jnp.where(inside, window, jnp.zeros_like(window)))
    return jnp.stack(copies, axis=1)


def back_conv(weight, rounded, pixel_side):
    channels = weight.shape[0]
    kernel = weight.reshape(channels, 9, channels)
    stacked = unfold_taps(rounded, pixel_side, -1)
    return jnp.einsum("okc,bkop->bcp", kernel, stacked, preferred_element_type=jnp.float32)


def advance(cotangent, rounded, layer_state, weight, step_size, pixel_side):
    activ = jnp.tanh(layer_state.astype(jnp.float32))
    return cotangent + step_size * (1.0 - activ * activ) * back_conv(weight, rounded, pixel_side)


def layer_grad(rounded, layer_state, pixel_side):
    activ = jnp.tanh(layer_state.astype(jnp.float32)).astype(jnp.bfloat16)
    stacked = unfold_taps(activ, pixel_side, 1)
    product = jnp.einsum("bop,bkcp->okc", rounded, stacked, preferred_element_type=jnp.float32)
    return (product * STEP).reshape(-1)


def shards(states, weights, guess, loss_cotangent):
    pixel_side = math.isqrt(states.shape[-1])
    sections = lax.axis_size("section")
    position = lax.axis_index("section")
    per_section = states.shape[0]
    initial = guess[0]
    relaxed = initial
    for layer_index in range(per_section - 1, -1, -1):
        relaxed = advance(
            relaxed,
            relaxed.astype(jnp.bfloat16),
            states[layer_index],
            weights[layer_index],
            STEP,
            pixel_side,
        )
    incoming = passed_along(relaxed, "section", -1)
    residual = jnp.where(position == sections - 1, loss_cotangent - initial, incoming - initial)
    coarse_size = per_section * STEP

    def coarse_round(round_index, running):
        carried = advance(
            running, running.astype(jnp.bfloat16), states[0], weights[0], coarse_size, pixel_side
        )
        return passed_along(carried, "section", -1) + residual

    correction = lax.fori_loop(0, sections - 1, coarse_round, residual)
    cotangent = initial + correction
    gradients = []
    for layer_index in range(per_section - 1, -1, -1):
        rounded = cotangent.astype(jnp.bfloat16)
        local_grad = layer_grad(rounded, states[layer_index], pixel_side)
        local_grad = lax.psum_scatter(local_grad, "batch", scatter_dimension=0, tiled=True)
        gradients.append(local_grad)
        cotangent = advance(
            cotangent, rounded, states[layer_index], weights[layer_index], STEP, pixel_side
        )
    stacked = jnp.stack(gradients[::-1], axis=0)
    return (cotangent[None], stacked)


def solution(mesh):
    placed = (
        P("section", "batch", None, None),
        P("section", None, None),
        P("section", "batch", None, None),
        P("batch", None, None),
    )
    return jax.shard_map(
        shards,
        mesh=mesh,
        in_specs=placed,
        out_specs=(P("section", "batch", None, None), P("section", "batch")),
        check_vma=False,
    )
```

profile of v0, /device:TPU:0, one launch (start us, length us, event | category | flops | bytes accessed | tf_op | source)
XLA Modules:
  0.0 192.5 jit_solution(13438125027563950923)
XLA Ops:
  7.2 1.2 fusion.35
  10.0 1.1 copy-done.2
  13.1 1.4 copy-done.5
  14.7 2.3 %fusion.52 = (bf16[2,64,1024]{2,1,0:T(8,128)(2,1)S(1)}, f32[2,64,1024]{2,1,0:T(8,128)S(1)}) fusion(bf16[64,9,64,1]{0,2,1,3:T(8,128)(2,1)S(1)} %bitcast.309, bf16[2,9,64,1024]{3,2,1,0:T(8,128)(2,1)} %copy-done.5, bf16[2,2,64,1024]{3,2,1,0:T(8,128)(2,1)S(1)} %copy-done, f32[1,2,64,1024]{3,2,1,0:T(8,128)S(1)} %copy-done.1), kind=kOutput, calls=%fused_computation.136 | convolution fusion | flops 151912448 | bytes 4005888 | tf_op jit(solution)/shard_map/okc,bkop->bcp/dot_general | solution.py:40
  17.0 1.1 bitcast_dynamic-update-slice_fusion.24
  19.0 0.9 bitcast_dynamic-update-slice_fusion.17
  20.1 1.0 bitcast_dynamic-update-slice_fusion.16
  21.7 1.4 copy-done.6
  23.3 2.4 %fusion.22 = f32[2,64,1024]{2,1,0:T(8,128)S(1)} fusion(f32[2,64,1024]{2,1,0:T(8,128)S(1)} %get-tuple-element.113, bf16[64,9,64,1]{0,2,3,1:T(8,128)(2,1)S(1)} %bitcast.311, bf16[2,9,64,1024]{3,2,0,1:T(8,128)(2,1)} %copy-done.6, bf16[2,2,64,1024]{3,2,1,0:T(8,128)(2,1)S(1)} %copy-done), kind=kOutput, calls=%fused_computation.37 | convolution fusion | flops 151781376 | bytes 3743744 | tf_op jit(solution)/shard_map/okc,bkop->bcp/dot_general | solution.py:40
  25.7 1.5 collective-permute-start.1
  29.7 88.5 %while.12 = (s32[]{:T(128)}, f32[2,64,1024]{2,1,0:T(8,128)S(1)}, bf16[2,2,64,1024]{3,2,1,0:T(8,128)(2,1)S(1)}, bf16[2,64,576]{1,2,0:T(8,128)(2,1)S(1)}, f32[2,64,1024]{2,1,0:T(8,128)S(1)}, /*index=5*/s32[]{:T(128)}) while((s32[]{:T(128)}, f32[2,64,1024]{2,1,0:T(8,128)S(1)}, bf16[2,2,64,1024]{3,2,1,0:T(8,128)(2,1)S(1)}, ...), condition=%wide.region_1.2_spmd, body=%wide.region_0.1_spmd.sunk | while | flops 153383936 | bytes 13340781 | solution.py:81
  31.6 1.3 collective-permute-start
  32.9 10.0 %collective-permute-done = f32[2,64,1024]{2,1,0:T(8,128)S(1)} collective-permute-done((f32[2,64,1024]{2,1,0:T(8,128)S(1)}, f32[2,64,1024]{2,1,0:T(8,128)S(1)}, u32[]{:S(2)}, u32[]{:S(2)}) %collective-permute-start) | collective-permute-done | bytes 524320 | tf_op jit(solution)/shard_map/while/body/eval_jaxpr/ppermute | solution.py:14
  45.0 1.3 collective-permute-start
  46.3 9.2 %collective-permute-done = f32[2,64,1024]{2,1,0:T(8,128)S(1)} collective-permute-done((f32[2,64,1024]{2,1,0:T(8,128)S(1)}, f32[2,64,1024]{2,1,0:T(8,128)S(1)}, u32[]{:S(2)}, u32[]{:S(2)}) %collective-permute-start) | collective-permute-done | bytes 524320 | tf_op jit(solution)/shard_map/while/body/eval_jaxpr/ppermute | solution.py:14
  57.5 1.3 collective-permute-start
  58.8 9.2 %collective-permute-done = f32[2,64,1024]{2,1,0:T(8,128)S(1)} collective-permute-done((f32[2,64,1024]{2,1,0:T(8,128)S(1)}, f32[2,64,1024]{2,1,0:T(8,128)S(1)}, u32[]{:S(2)}, u32[]{:S(2)}) %collective-permute-start) | collective-permute-done | bytes 524320 | tf_op jit(solution)/shard_map/while/body/eval_jaxpr/ppermute | solution.py:14
  70.0 1.3 collective-permute-start
  71.3 9.2 %collective-permute-done = f32[2,64,1024]{2,1,0:T(8,128)S(1)} collective-permute-done((f32[2,64,1024]{2,1,0:T(8,128)S(1)}, f32[2,64,1024]{2,1,0:T(8,128)S(1)}, u32[]{:S(2)}, u32[]{:S(2)}) %collective-permute-start) | collective-permute-done | bytes 524320 | tf_op jit(solution)/shard_map/while/body/eval_jaxpr/ppermute | solution.py:14
  82.5 1.3 collective-permute-start
  83.8 9.2 %collective-permute-done = f32[2,64,1024]{2,1,0:T(8,128)S(1)} collective-permute-done((f32[2,64,1024]{2,1,0:T(8,128)S(1)}, f32[2,64,1024]{2,1,0:T(8,128)S(1)}, u32[]{:S(2)}, u32[]{:S(2)}) %collective-permute-start) | collective-permute-done | bytes 524320 | tf_op jit(solution)/shard_map/while/body/eval_jaxpr/ppermute | solution.py:14
  95.0 1.3 collective-permute-start
  96.3 9.2 %collective-permute-done = f32[2,64,1024]{2,1,0:T(8,128)S(1)} collective-permute-done((f32[2,64,1024]{2,1,0:T(8,128)S(1)}, f32[2,64,1024]{2,1,0:T(8,128)S(1)}, u32[]{:S(2)}, u32[]{:S(2)}) %collective-permute-start) | collective-permute-done | bytes 524320 | tf_op jit(solution)/shard_map/while/body/eval_jaxpr/ppermute | solution.py:14
  107.6 1.3 collective-permute-start
  108.9 9.2 %collective-permute-done = f32[2,64,1024]{2,1,0:T(8,128)S(1)} collective-permute-done((f32[2,64,1024]{2,1,0:T(8,128)S(1)}, f32[2,64,1024]{2,1,0:T(8,128)S(1)}, u32[]{:S(2)}, u32[]{:S(2)}) %collective-permute-start) | collective-permute-done | bytes 524320 | tf_op jit(solution)/shard_map/while/body/eval_jaxpr/ppermute | solution.py:14
  121.1 1.2 fusion.26
  123.3 2.8 %fusion.25 = f32[64,9,64]{2,0,1:T(8,128)S(1)} fusion(bf16[2,9,64,1024]{3,2,0,1:T(8,128)(2,1)} %get-tuple-element.108, bf16[2,64,1024]{2,1,0:T(8,128)(2,1)S(1)} %fusion.36), kind=kOutput, calls=%fused_computation.42 | convolution fusion | flops 151031808 | bytes 2768896 | tf_op jit(solution)/shard_map/bop,bkcp->okc/dot_general | solution.py:51
  127.1 0.9 bitcast_dynamic-update-slice_fusion.39
  128.0 0.9 bitcast_dynamic-update-slice_fusion.38
  132.1 0.9 bitcast_dynamic-update-slice_fusion.33
  133.8 3.1 %fusion.18 = f32[1,2,64,1024]{3,2,1,0:T(8,128)} fusion(f32[2,64,1024]{2,1,0:T(8,128)S(1)} %get-tuple-element.115, bf16[64,9,64,1]{0,2,3,1:T(8,128)(2,1)S(1)} %bitcast.312, bf16[2,9,64,1024]{3,2,0,1:T(8,128)(2,1)} %bitcast_dynamic-update-slice_fusion.32, bf16[2,2,64,1024]{3,2,1,0:T(8,128)(2,1)S(1)} %get-tuple-element.169), kind=kOutput, calls=%fused_computation.31 | convolution fusion | flops 151781376 | bytes 3743744 | tf_op jit(solution)/shard_map/okc,bkop->bcp/dot_general | solution.py:40
  136.9 46.5 %all-reduce.12.cloned.1.call-done = (f32[36864]{0:T(1024)}, f32[36864]{0:T(1024)}) async-done(((f32[36864]{0:T(1024)}, f32[36864]{0:T(1024)}), (f32[36864]{0:T(1024)}, f32[36864]{0:T(1024)})) %all-reduce.12.cloned.1.call-update) | async-done | bytes 294928
  (202 shorter events, 31.5 us)
Async XLA Ops:
  7.2 176.3 %all-reduce.12.cloned.1.call-start = ((), (), s32[]{:S(2)}) async-start(), calls=%async_computation | async-start | bytes 589824
  8.4 1.2 copy-start
  9.1 2.2 %copy-start.1 = (f32[1,2,64,1024]{3,2,1,0:T(8,128)S(1)}, f32[1,2,64,1024]{3,2,1,0:T(8,128)}, u32[]{:S(2)}) copy-start(f32[1,2,64,1024]{3,2,1,0:T(8,128)} %param.8) | copy-start | bytes 1572868
  9.7 1.4 copy-start.2
  11.3 1.4 copy-start.3
  11.5 3.0 %copy-start.11 = (bf16[2,64,576]{2,1,0:T(8,128)(2,1)S(1)}, bf16[2,64,576]{2,1,0:T(8,128)(2,1)}, u32[]{:S(2)}) copy-start(bf16[2,64,576]{2,1,0:T(8,128)(2,1)} %param.7) | copy-start | bytes 442372
  13.1 1.4 copy-start.5
  14.7 3.5 %copy-start.7 = (bf16[1,64,576]{1,2,0:T(8,128)(2,1)}, bf16[1,64,576]{1,2,0:T(8,128)(2,1)S(1)}, u32[]{:S(2)}) copy-start(bf16[1,64,576]{1,2,0:T(8,128)(2,1)S(1)} %copy.68) | copy-start | bytes 221188
  21.7 1.4 copy-start.6
  23.2 4.2 %copy-start.13 = (u32[32]{0:T(128)S(1)}, u32[32]{0:T(128)}, u32[]{:S(2)}) copy-start(u32[32]{0:T(128)} %constant.131) | copy-start | bytes 388
  23.2 6.3 %copy-start.12 = (f32[2,64,1024]{2,1,0:T(8,128)S(1)}, f32[2,64,1024]{2,1,0:T(8,128)}, u32[]{:S(2)}) copy-start(f32[2,64,1024]{2,1,0:T(8,128)} %param.9) | copy-start | bytes 1572868
  23.3 3.9 %copy-start.9 = (bf16[1,64,576]{1,2,0:T(8,128)(2,1)}, bf16[1,64,576]{1,2,0:T(8,128)(2,1)S(1)}, u32[]{:S(2)}) copy-start(bf16[1,64,576]{1,2,0:T(8,128)(2,1)S(1)} %copy.69) | copy-start | bytes 221188
  25.7 3.8 %collective-permute-start.1 = (f32[2,64,1024]{2,1,0:T(8,128)S(1)}, f32[2,64,1024]{2,1,0:T(8,128)S(1)}, u32[]{:S(2)}, u32[]{:S(2)}) collective-permute-start(f32[2,64,1024]{2,1,0:T(8,128)S(1)} %fusion.22), channel_id=1, source_target_pairs={{4,0},{8,4},{12,8},{16,12},{20,16},{24,20},{28,24},{5,1},{9,5},{13... | collective-permute-start | bytes 1572872 | tf_op jit(solution)/shard_map/ppermute | solution.py:14
  31.6 11.3 %collective-permute-start = (f32[2,64,1024]{2,1,0:T(8,128)S(1)}, f32[2,64,1024]{2,1,0:T(8,128)S(1)}, u32[]{:S(2)}, u32[]{:S(2)}) collective-permute-start(f32[2,64,1024]{2,1,0:T(8,128)S(1)} %fusion.77), channel_id=1, source_target_pairs={{4,0},{8,4},{12,8},{16,12},{20,16},{24,20},{28,24},{5,1},{9,5},{13... | collective-permute-start | bytes 1572872 | tf_op jit(solution)/shard_map/while/body/eval_jaxpr/ppermute | solution.py:14
  45.0 10.5 %collective-permute-start = (f32[2,64,1024]{2,1,0:T(8,128)S(1)}, f32[2,64,1024]{2,1,0:T(8,128)S(1)}, u32[]{:S(2)}, u32[]{:S(2)}) collective-permute-start(f32[2,64,1024]{2,1,0:T(8,128)S(1)} %fusion.77), channel_id=1, source_target_pairs={{4,0},{8,4},{12,8},{16,12},{20,16},{24,20},{28,24},{5,1},{9,5},{13... | collective-permute-start | bytes 1572872 | tf_op jit(solution)/shard_map/while/body/eval_jaxpr/ppermute | solution.py:14
  57.5 10.5 %collective-permute-start = (f32[2,64,1024]{2,1,0:T(8,128)S(1)}, f32[2,64,1024]{2,1,0:T(8,128)S(1)}, u32[]{:S(2)}, u32[]{:S(2)}) collective-permute-start(f32[2,64,1024]{2,1,0:T(8,128)S(1)} %fusion.77), channel_id=1, source_target_pairs={{4,0},{8,4},{12,8},{16,12},{20,16},{24,20},{28,24},{5,1},{9,5},{13... | collective-permute-start | bytes 1572872 | tf_op jit(solution)/shard_map/while/body/eval_jaxpr/ppermute | solution.py:14
  70.0 10.5 %collective-permute-start = (f32[2,64,1024]{2,1,0:T(8,128)S(1)}, f32[2,64,1024]{2,1,0:T(8,128)S(1)}, u32[]{:S(2)}, u32[]{:S(2)}) collective-permute-start(f32[2,64,1024]{2,1,0:T(8,128)S(1)} %fusion.77), channel_id=1, source_target_pairs={{4,0},{8,4},{12,8},{16,12},{20,16},{24,20},{28,24},{5,1},{9,5},{13... | collective-permute-start | bytes 1572872 | tf_op jit(solution)/shard_map/while/body/eval_jaxpr/ppermute | solution.py:14
  82.5 10.5 %collective-permute-start = (f32[2,64,1024]{2,1,0:T(8,128)S(1)}, f32[2,64,1024]{2,1,0:T(8,128)S(1)}, u32[]{:S(2)}, u32[]{:S(2)}) collective-permute-start(f32[2,64,1024]{2,1,0:T(8,128)S(1)} %fusion.77), channel_id=1, source_target_pairs={{4,0},{8,4},{12,8},{16,12},{20,16},{24,20},{28,24},{5,1},{9,5},{13... | collective-permute-start | bytes 1572872 | tf_op jit(solution)/shard_map/while/body/eval_jaxpr/ppermute | solution.py:14
  95.0 10.5 %collective-permute-start = (f32[2,64,1024]{2,1,0:T(8,128)S(1)}, f32[2,64,1024]{2,1,0:T(8,128)S(1)}, u32[]{:S(2)}, u32[]{:S(2)}) collective-permute-start(f32[2,64,1024]{2,1,0:T(8,128)S(1)} %fusion.77), channel_id=1, source_target_pairs={{4,0},{8,4},{12,8},{16,12},{20,16},{24,20},{28,24},{5,1},{9,5},{13... | collective-permute-start | bytes 1572872 | tf_op jit(solution)/shard_map/while/body/eval_jaxpr/ppermute | solution.py:14
  107.6 10.5 %collective-permute-start = (f32[2,64,1024]{2,1,0:T(8,128)S(1)}, f32[2,64,1024]{2,1,0:T(8,128)S(1)}, u32[]{:S(2)}, u32[]{:S(2)}) collective-permute-start(f32[2,64,1024]{2,1,0:T(8,128)S(1)} %fusion.77), channel_id=1, source_target_pairs={{4,0},{8,4},{12,8},{16,12},{20,16},{24,20},{28,24},{5,1},{9,5},{13... | collective-permute-start | bytes 1572872 | tf_op jit(solution)/shard_map/while/body/eval_jaxpr/ppermute | solution.py:14
  118.2 1.2 copy-start.8
  119.5 1.7 copy-start.4
  127.1 6.7 %copy-start.10 = (bf16[1,64,576]{1,2,0:T(8,128)(2,1)S(1)}, bf16[1,64,576]{1,2,0:T(8,128)(2,1)}, u32[]{:S(2)}) copy-start(bf16[1,64,576]{1,2,0:T(8,128)(2,1)} %copy-done.9) | copy-start | bytes 221188
Sparse Core Ops, SparseCore 0:
  133.1 50.2 all-reduce.11
where the time goes:
time: 193 us
  waiting for transfers between devices  113 us (59%)
  other arithmetic  27 us (14%)
  matrix products  16.8 us (9%)
  between operations  15.2 us (8%)
  starting transfers between devices  10.6 us (5%)
  local copies, waits for them, and re-layouts  9.44 us (5%)
    ppermute x8, waiting for transfers between devices, passed_along(): return lax.ppermute(block, axis, route)  66 us
    unnamed x2, waiting for transfers between devices  46.5 us
    dot_general x11, matrix products, back_conv(): jnp.einsum('okc,bkop->bcp', kernel, stacked, preferred_element_type=jnp.f...  12.8 us
    unnamed x42, other arithmetic  12.8 us
    ppermute x8, starting transfers between devices, passed_along(): return lax.ppermute(block, axis, route)  10.5 us
    while x56, other arithmetic  7.06 us
    unnamed x32, local copies, waits for them, and re-layouts  6.93 us
    another operation x13, other arithmetic, unfold_taps(): return jnp.stack(copies, axis=1)  4.34 us
  transfers between devices with their start and end apart: 9, of which 9 were waited for; matrix products, arithmetic and copies ran while one was open for 2% of the time, Pallas kernels for 0%

commit v1 on v0

v1 whole, which is shorter than its diff:
```python
import functools
import math

import jax
import jax.numpy as jnp
from jax import lax
from jax.experimental import pallas as pl
from jax.experimental.pallas import tpu as pltpu
from jax.sharding import PartitionSpec as P

STEP = 0.0625
CHUNKS = 4
MESH = pl.DeviceIdType.MESH


def kernel(
    sections, groups, side,
    states_ref, weights_ref, guess_ref, loss_ref, start_ref, grads_ref,
    wide, blocks, scaled, held, base, incoming, outgoing, taps, acts, parts, landed,
    send_sem, recv_sem, part_send, part_recv,
):
    position = lax.axis_index("section")
    member = lax.axis_index("batch")
    layers = states_ref.shape[0]
    lanes, length = guess_ref.shape
    channels = weights_ref.shape[1]
    size = length // CHUNKS
    f32, bf16 = jnp.float32, jnp.bfloat16

    barrier = pltpu.get_barrier_semaphore()

    @pl.when(position > 0)
    def _():
        pl.semaphore_signal(
            barrier, inc=1, device_id={"section": position - 1}, device_id_type=MESH
        )

    @pl.when(position < sections - 1)
    def _():
        pl.semaphore_signal(
            barrier, inc=1, device_id={"section": position + 1}, device_id_type=MESH
        )

    for offset in range(1, groups):
        pl.semaphore_signal(
            barrier,
            inc=1,
            device_id={"batch": lax.rem(member + offset, groups)},
            device_id_type=MESH,
        )

    column = lax.broadcasted_iota(jnp.int32, (size, lanes), 0) % side
    not_first = column > 0
    not_last = column < side - 1
    low = lax.broadcasted_iota(jnp.int32, (channels, lanes), 1) < channels

    def shifted(values):
        before = jnp.where(not_first, pltpu.roll(values, 1, 0), 0.0)
        after = jnp.where(not_last, pltpu.roll(values, size - 1, 0), 0.0)
        return before.astype(bf16), values.astype(bf16), after.astype(bf16)

    def put_taps(first, values):
        before, same, after = shifted(values)
        rows = pl.ds(first + side, size)
        taps[rows, 0:lanes] = after
        taps[rows, lanes : 2 * lanes] = same
        taps[rows, 2 * lanes : 3 * lanes] = before

    def conv(layer, first):
        stacked = jnp.concatenate(
            [taps[pl.ds(first + side - a * side, size), :] for a in (-1, 0, 1)], axis=1
        )
        return jnp.dot(stacked, blocks[layer], preferred_element_type=f32)

    def prepare_weights(layer):
        wide[:, 9 * channels :] = jnp.zeros((channels, wide.shape[1] - 9 * channels), f32)
        wide[:, 0 : 9 * channels] = weights_ref[layer].astype(f32)
        for k in range(9):
            pair = wide[:, (k // 2) * lanes : (k // 2 + 1) * lanes]
            turned = pltpu.roll(pair, channels, 1)
            left, right = (pair, turned) if k % 2 == 0 else (turned, pair)
            blocks[layer, k * lanes : k * lanes + channels, :] = jnp.where(
                low, left, 0.0
            ).astype(bf16)
            blocks[layer, k * lanes + channels : (k + 1) * lanes, :] = jnp.where(
                low, 0.0, right
            ).astype(bf16)

    def prepare_state(layer):
        activ = jnp.tanh(states_ref[layer].astype(f32)).T
        scaled[layer] = STEP * (1.0 - activ * activ)
        edge = jnp.zeros((side, 3 * lanes), bf16)
        acts[layer, 0:side, :] = edge
        acts[layer, side + length :, :] = edge
        for i in range(CHUNKS):
            before, same, after = shifted(activ[i * size : (i + 1) * size])
            rows = slice(side + i * size, side + (i + 1) * size)
            acts[layer, rows, 0:lanes] = before
            acts[layer, rows, lanes : 2 * lanes] = same
            acts[layer, rows, 2 * lanes :] = after

    edge = jnp.zeros((side, 3 * lanes), bf16)
    taps[0:side, :] = edge
    taps[side + length :, :] = edge
    for layer in range(layers):
        prepare_weights(layer)
        prepare_state(layer)

    @pl.when(position == sections - 1)
    def _():
        incoming[...] = loss_ref[...].T

    held[...] = guess_ref[...].T

    base[...] = jnp.zeros_like(base)
    for layer in range(layers - 1, -1, -1):
        for i in range(CHUNKS):
            rows = slice(i * size, (i + 1) * size)
            put_taps(i * size, held[rows, :] + base[rows, :])
        for i in range(CHUNKS):
            rows = slice(i * size, (i + 1) * size)
            base[rows, :] += scaled[layer, rows, :] * conv(layer, i * size)

    neighbours = (
        groups - 1
        + (position > 0).astype(jnp.int32)
        + (position < sections - 1).astype(jnp.int32)
    )
    pl.semaphore_wait(barrier, neighbours)

    def hop(i):
        rows = pl.ds(i * size, size)
        return pltpu.make_async_remote_copy(
            src_ref=outgoing.at[rows, :],
            dst_ref=incoming.at[rows, :],
            send_sem=send_sem.at[i],
            recv_sem=recv_sem.at[i],
            device_id={"section": position - 1},
            device_id_type=MESH,
        )

    def carry(i):
        rows = slice(i * size, (i + 1) * size)
        outgoing[rows, :] = (
            incoming[rows, :] + base[rows, :]
            + layers * scaled[0, rows, :] * conv(0, i * size)
        )
        hop(i).start()

    for i in range(CHUNKS):
        @pl.when(position < sections - 1)
        def _():
            hop(i).wait_recv()

        @pl.when(position > 0)
        def _():
            rows = slice(i * size, (i + 1) * size)
            put_taps(i * size, incoming[rows, :] - held[rows, :])
            if i > 0:
                carry(i - 1)

    @pl.when(position > 0)
    def _():
        carry(CHUNKS - 1)

    def share(layer, offset):
        peer = lax.rem(member + offset, groups)
        return pltpu.make_async_remote_copy(
            src_ref=parts.at[layer, peer],
            dst_ref=landed.at[layer, offset - 1],
            send_sem=part_send.at[layer, offset - 1],
            recv_sem=part_recv.at[layer, offset - 1],
            device_id={"batch": peer},
            device_id_type=MESH,
        )

    for layer in range(layers - 1, -1, -1):
        turned_lam = incoming[...].T.astype(bf16)
        sums = []
        for a in (-1, 0, 1):
            first = side + a * side
            sums.append(
                jnp.dot(
                    turned_lam,
                    acts[layer, first : first + length, :],
                    preferred_element_type=f32,
                )
            )
        pieces = [sums[k // 3][:, (k % 3) * lanes : (k % 3 + 1) * lanes] for k in range(9)]
        held_rows = channels // groups
        for k in range(0, 9, 2):
            even = pieces[k][:channels] + pltpu.roll(pieces[k][channels:], channels, 1)
            if k < 8:
                odd = pltpu.roll(pieces[k + 1][:channels], channels, 1) + pieces[k + 1][channels:]
                both = jnp.where(low, even, odd) * STEP
                width = lanes
            else:
                both = even[:, :channels] * STEP
                width = channels
            for g in range(groups):
                parts[layer, g, :, k * channels : k * channels + width] = both[
                    g * held_rows : (g + 1) * held_rows
                ]
        for offset in range(1, groups):
            share(layer, offset).start()

        for i in range(CHUNKS):
            put_taps(i * size, incoming[i * size : (i + 1) * size, :])
        for i in range(CHUNKS):
            rows = slice(i * size, (i + 1) * size)
            incoming[rows, :] += scaled[layer, rows, :] * conv(layer, i * size)

    start_ref[...] = incoming[...].T

    for layer in range(layers - 1, -1, -1):
        total = parts[layer, member]
        for offset in range(1, groups):
            share(layer, offset).wait_recv()
            total = total + landed[layer, offset - 1]
        grads_ref[layer] = total
        for offset in range(1, groups):
            share(layer, offset).wait_send()

    @pl.when(position > 0)
    def _():
        for i in range(CHUNKS):
            hop(i).wait_send()


def shards(states, weights, guess, loss_cotangent):
    sections = lax.axis_size("section")
    groups = lax.axis_size("batch")
    layers, images, channels, length = states.shape
    side = math.isqrt(length)
    lanes = images * channels
    rows = channels // groups
    f32, bf16 = jnp.float32, jnp.bfloat16
    start, grads = pl.pallas_call(
        functools.partial(kernel, sections, groups, side),
        out_shape=(
            jax.ShapeDtypeStruct((lanes, length), f32),
            jax.ShapeDtypeStruct((layers, rows, 9 * channels), f32),
        ),
        in_specs=[pl.BlockSpec(memory_space=pltpu.VMEM)] * 4,
        out_specs=(pl.BlockSpec(memory_space=pltpu.VMEM),) * 2,
        scratch_shapes=[
            pltpu.VMEM((channels, 5 * lanes), f32),
            pltpu.VMEM((layers, 9 * lanes, lanes), bf16),
            pltpu.VMEM((layers, length, lanes), f32),
            pltpu.VMEM((length, lanes), f32),
            pltpu.VMEM((length, lanes), f32),
            pltpu.VMEM((length, lanes), f32),
            pltpu.VMEM((length, lanes), f32),
            pltpu.VMEM((length + 2 * side, 3 * lanes), bf16),
            pltpu.VMEM((layers, length + 2 * side, 3 * lanes), bf16),
            pltpu.VMEM((layers, groups, rows, 9 * channels), f32),
            pltpu.VMEM((layers, groups - 1, rows, 9 * channels), f32),
            pltpu.SemaphoreType.DMA((CHUNKS,)),
            pltpu.SemaphoreType.DMA((CHUNKS,)),
            pltpu.SemaphoreType.DMA((layers, groups - 1)),
            pltpu.SemaphoreType.DMA((layers, groups - 1)),
        ],
        compiler_params=pltpu.CompilerParams(
            collective_id=0, has_side_effects=True, vmem_limit_bytes=40 * 2**20
        ),
    )(
        states.reshape(layers, lanes, length),
        weights,
        guess.reshape(lanes, length),
        loss_cotangent.reshape(lanes, length),
    )
    return start.reshape(guess.shape), grads.reshape(layers, rows * 9 * channels)


def solution(mesh):
    placed = (
        P("section", "batch", None, None),
        P("section", None, None),
        P("section", "batch", None, None),
        P("batch", None, None),
    )
    return jax.shard_map(
        shards,
        mesh=mesh,
        in_specs=placed,
        out_specs=(P("section", "batch", None, None), P("section", "batch")),
        check_vma=False,
    )
```

time: 193 us -> 49.1 us (0.25)
  waiting for transfers between devices: 113 us -> 0 us
  Pallas kernels: 0 us -> 42.6 us
  other arithmetic: 27 us -> 0 us
  matrix products: 16.8 us -> 0 us
  between operations: 15.2 us -> 0.65 us
  starting transfers between devices: 10.6 us -> 0 us
  local copies, waits for them, and re-layouts: 9.44 us -> 5.57 us
    ppermute x8 -> x0, waiting for transfers between devices: 66 us -> none  [passed_along(): return lax.ppermute(block, axis, route)]
    unnamed x2 -> x0, waiting for transfers between devices: 46.5 us -> none
    pallas_call x0 -> x1, Pallas kernels: none -> 42.6 us  [shards(): pl.pallas_call(functools.partial(kernel, sections, groups, side), out_sha...]
    dot_general x13 -> x0, matrix products: 16.8 us -> none  [the longest x11 12.8 us: back_conv(): jnp.einsum('okc,bkop->bcp', kernel, stacked, preferred_element_type=jnp.f...]
    unnamed x42 -> x0, other arithmetic: 12.8 us -> none
    ppermute x8 -> x0, starting transfers between devices: 10.5 us -> none  [passed_along(): return lax.ppermute(block, axis, route)]
    while x56 -> x0, other arithmetic: 7.06 us -> none
    another operation x14 -> x0, other arithmetic: 5.04 us -> none  [the longest x13 4.34 us: unfold_taps(): return jnp.stack(copies, axis=1)]
  transfers between devices with their start and end apart: 9 -> 0, of which waited for: 9 -> 0; matrix products, arithmetic and copies ran while one was open for 2% -> 0% of each run, Pallas kernels for 0% -> 0%
where the time goes in v1:
time: 49.1 us; the launch traced here: 48.8 us
  Pallas kernels  42.6 us (87%)
  local copies, waits for them, and re-layouts  5.57 us (11%)
  between operations  0.65 us (1%)
    pallas_call x1, Pallas kernels, shards(): pl.pallas_call(functools.partial(kernel, sections, groups, side), out_sha...  42.6 us
    unnamed x9, local copies, waits for them, and re-layouts  4.82 us

profile of v1, /device:TPU:0, one launch (start us, length us, event | category | flops | bytes accessed | tf_op | source)
XLA Modules:
  0.0 48.8 jit_solution(12593858954034186760)
XLA Ops:
  0.6 0.0 copy-start
  0.6 1.0 %copy-done = bf16[2,2,64,1024]{3,2,1,0:T(8,128)(2,1)S(1)} copy-done((bf16[2,2,64,1024]{3,2,1,0:T(8,128)(2,1)S(1)}, bf16[2,2,64,1024]{3,2,1,0:T(8,128)(2,1)}, u32[]{:S(2)}) %copy-start) | copy-done | bytes 524312
  1.7 0.0 copy-start.1
  1.7 1.0 %copy-done.1 = f32[1,2,64,1024]{3,2,1,0:T(8,128)S(1)} copy-done((f32[1,2,64,1024]{3,2,1,0:T(8,128)S(1)}, f32[1,2,64,1024]{3,2,1,0:T(8,128)}, u32[]{:S(2)}) %copy-start.1) | copy-done | bytes 524312
  2.7 0.0 copy-start.2
  2.7 1.0 %copy-done.2 = f32[2,64,1024]{2,1,0:T(8,128)S(1)} copy-done((f32[2,64,1024]{2,1,0:T(8,128)S(1)}, f32[2,64,1024]{2,1,0:T(8,128)}, u32[]{:S(2)}) %copy-start.2) | copy-done | bytes 524312
  3.8 0.0 copy-start.3
  3.8 0.9 %copy-done.3 = bf16[2,64,576]{2,1,0:T(8,128)(2,1)S(1)} copy-done((bf16[2,64,576]{2,1,0:T(8,128)(2,1)S(1)}, bf16[2,64,576]{2,1,0:T(8,128)(2,1)}, u32[]{:S(2)}) %copy-start.3) | copy-done | bytes 147480
  4.7 42.6 %shard_map.59 = (f32[128,1024]{1,0:T(8,128)S(1)}, f32[2,16,576]{2,1,0:T(8,128)S(1)}) custom-call(bf16[2,128,1024]{2,1,0:T(8,128)(2,1)S(1)} %bitcast.4, bf16[2,64,576]{2,1,0:T(8,128)(2,1)S(1)} %copy-done.3, f32[128,1024]{1,0:T(8,128)S(1)} %bitcast.5, f32[128,1024]{1,0:T(8,128)S(1)} %bitcast.6), custom_call_target="tpu_custom_call" | custom-call | tf_op jit(solution)/shard_map/pallas_call | solution.py:238
  47.3 0.7 %reshape.23 = f32[2,9216]{1,0:T(2,128)} reshape(f32[2,16,576]{2,1,0:T(8,128)S(1)} %get-tuple-element.5) | data formatting | bytes 147456 | tf_op jit(solution)/shard_map/reshape | solution.py:272
  48.1 0.8 %copy.7 = f32[1,2,64,1024]{3,2,1,0:T(8,128)} copy(f32[1,2,64,1024]{3,2,1,0:T(8,128)S(1)} %bitcast.7) | data formatting | bytes 1048576
Async XLA Ops:
  0.6 1.0 %copy-start = (bf16[2,2,64,1024]{3,2,1,0:T(8,128)(2,1)S(1)}, bf16[2,2,64,1024]{3,2,1,0:T(8,128)(2,1)}, u32[]{:S(2)}) copy-start(bf16[2,2,64,1024]{3,2,1,0:T(8,128)(2,1)} %param.4) | copy-start | bytes 1572868
  1.7 1.0 %copy-start.1 = (f32[1,2,64,1024]{3,2,1,0:T(8,128)S(1)}, f32[1,2,64,1024]{3,2,1,0:T(8,128)}, u32[]{:S(2)}) copy-start(f32[1,2,64,1024]{3,2,1,0:T(8,128)} %param.6) | copy-start | bytes 1572868
  2.7 1.0 %copy-start.2 = (f32[2,64,1024]{2,1,0:T(8,128)S(1)}, f32[2,64,1024]{2,1,0:T(8,128)}, u32[]{:S(2)}) copy-start(f32[2,64,1024]{2,1,0:T(8,128)} %param.7) | copy-start | bytes 1572868
  3.8 0.9 %copy-start.3 = (bf16[2,64,576]{2,1,0:T(8,128)(2,1)S(1)}, bf16[2,64,576]{2,1,0:T(8,128)(2,1)}, u32[]{:S(2)}) copy-start(bf16[2,64,576]{2,1,0:T(8,128)(2,1)} %weights_ref.1) | copy-start | bytes 442372

commit v2 on v1

--- a/solution.py
+++ b/solution.py
@@ -9,23 +9,36 @@
 from jax.sharding import PartitionSpec as P
 
 STEP = 0.0625
-CHUNKS = 4
+PIECES = 4
+CHUNKS = 8
+FLYING = 2
 MESH = pl.DeviceIdType.MESH
 
 
 def kernel(
     sections, groups, side,
-    states_ref, weights_ref, guess_ref, loss_ref, start_ref, grads_ref,
-    wide, blocks, scaled, held, base, incoming, outgoing, taps, acts, parts, landed,
-    send_sem, recv_sem, part_send, part_recv,
+    states_hbm, weights_hbm, guess_hbm, loss_hbm, start_ref, grads_ref,
+    states_ref, weights_ref, guess_ref, loss_ref,
+    wide, blocks, scaled, held, base, incoming, outgoing, taps, acts, parts, sent, landed,
+    send_sem, recv_sem, part_send, part_recv, load_sem,
 ):
     position = lax.axis_index("section")
     member = lax.axis_index("batch")
     layers = states_ref.shape[0]
     lanes, length = guess_ref.shape
     channels = weights_ref.shape[1]
-    size = length // CHUNKS
+    size, part = length // CHUNKS, length // PIECES
     f32, bf16 = jnp.float32, jnp.bfloat16
+
+    loads = [
+        pltpu.make_async_copy(source, target, load_sem.at[n])
+        for n, (source, target) in enumerate(
+            ((weights_hbm, weights_ref), (states_hbm, states_ref),
+             (guess_hbm, guess_ref), (loss_hbm, loss_ref))
+        )
+    ]
+    for load in loads:
+        load.start()
 
     barrier = pltpu.get_barrier_semaphore()
 
@@ -49,26 +62,27 @@
             device_id_type=MESH,
         )
 
-    column = lax.broadcasted_iota(jnp.int32, (size, lanes), 0) % side
+    column = lax.broadcasted_iota(jnp.int32, (part, lanes), 0) % side
     not_first = column > 0
     not_last = column < side - 1
     low = lax.broadcasted_iota(jnp.int32, (channels, lanes), 1) < channels
 
     def shifted(values):
-        before = jnp.where(not_first, pltpu.roll(values, 1, 0), 0.0)
-        after = jnp.where(not_last, pltpu.roll(values, size - 1, 0), 0.0)
+        count = values.shape[0]
+        before = jnp.where(not_first[:count], pltpu.roll(values, 1, 0), 0.0)
+        after = jnp.where(not_last[:count], pltpu.roll(values, count - 1, 0), 0.0)
         return before.astype(bf16), values.astype(bf16), after.astype(bf16)
 
     def put_taps(first, values):
         before, same, after = shifted(values)
-        rows = pl.ds(first + side, size)
+        rows = pl.ds(first + side, values.shape[0])
         taps[rows, 0:lanes] = after
         taps[rows, lanes : 2 * lanes] = same
         taps[rows, 2 * lanes : 3 * lanes] = before
 
-    def conv(layer, first):
+    def conv(layer, first, count):
         stacked = jnp.concatenate(
-            [taps[pl.ds(first + side - a * side, size), :] for a in (-1, 0, 1)], axis=1
+            [taps[pl.ds(first + side - a * side, count), :] for a in (-1, 0, 1)], axis=1
         )
         return jnp.dot(stacked, blocks[layer], preferred_element_type=f32)
 
@@ -89,12 +103,15 @@
     def prepare_state(layer):
         activ = jnp.tanh(states_ref[layer].astype(f32)).T
         scaled[layer] = STEP * (1.0 - activ * activ)
+
+    def prepare_acts(layer):
+        activ = jnp.tanh(states_ref[layer].astype(f32)).T
         edge = jnp.zeros((side, 3 * lanes), bf16)
         acts[layer, 0:side, :] = edge
         acts[layer, side + length :, :] = edge
-        for i in range(CHUNKS):
-            before, same, after = shifted(activ[i * size : (i + 1) * size])
-            rows = slice(side + i * size, side + (i + 1) * size)
+        for i in range(PIECES):
+            before, same, after = shifted(activ[i * part : (i + 1) * part])
+            rows = slice(side + i * part, side + (i + 1) * part)
             acts[layer, rows, 0:lanes] = before
             acts[layer, rows, lanes : 2 * lanes] = same
             acts[layer, rows, 2 * lanes :] = after
@@ -102,9 +119,14 @@
     edge = jnp.zeros((side, 3 * lanes), bf16)
     taps[0:side, :] = edge
     taps[side + length :, :] = edge
+    loads[0].wait()
     for layer in range(layers):
         prepare_weights(layer)
+    loads[1].wait()
+    for layer in range(layers):
         prepare_state(layer)
+    loads[2].wait()
+    loads[3].wait()
 
     @pl.when(position == sections - 1)
     def _():
@@ -114,12 +136,17 @@
 
     base[...] = jnp.zeros_like(base)
     for layer in range(layers - 1, -1, -1):
-        for i in range(CHUNKS):
-            rows = slice(i * size, (i + 1) * size)
-            put_taps(i * size, held[rows, :] + base[rows, :])
-        for i in range(CHUNKS):
-            rows = slice(i * size, (i + 1) * size)
-            base[rows, :] += scaled[layer, rows, :] * conv(layer, i * size)
+        for i in range(PIECES):
+            rows = slice(i * part, (i + 1) * part)
+            put_taps(i * part, held[rows, :] + base[rows, :])
+        for i in range(PIECES):
+            rows = slice(i * part, (i + 1) * part)
+            base[rows, :] += scaled[layer, rows, :] * conv(layer, i * part, part)
+
+    @pl.when(position < sections - 1)
+    def _():
+        for layer in range(layers):
+            prepare_acts(layer)
 
     neighbours = (
         groups - 1
@@ -143,8 +170,10 @@
         rows = slice(i * size, (i + 1) * size)
         outgoing[rows, :] = (
             incoming[rows, :] + base[rows, :]
-            + layers * scaled[0, rows, :] * conv(0, i * size)
-        )
+            + layers * scaled[0, rows, :] * conv(0, i * size, size)
+        )
+        if i >= FLYING:
+            hop(i - FLYING).wait_send()
         hop(i).start()
 
     for i in range(CHUNKS):
@@ -163,10 +192,15 @@
     def _():
         carry(CHUNKS - 1)
 
+    @pl.when(position == sections - 1)
+    def _():
+        for layer in range(layers):
+            prepare_acts(layer)
+
     def share(layer, offset):
         peer = lax.rem(member + offset, groups)
         return pltpu.make_async_remote_copy(
-            src_ref=parts.at[layer, peer],
+            src_ref=sent.at[layer, peer],
             dst_ref=landed.at[layer, offset - 1],
             send_sem=part_send.at[layer, offset - 1],
             recv_sem=part_recv.at[layer, offset - 1],
@@ -198,17 +232,18 @@
                 both = even[:, :channels] * STEP
                 width = channels
             for g in range(groups):
-                parts[layer, g, :, k * channels : k * channels + width] = both[
-                    g * held_rows : (g + 1) * held_rows
-                ]
+                share_of = both[g * held_rows : (g + 1) * held_rows]
+                columns = slice(k * channels, k * channels + width)
+                parts[layer, g, :, columns] = share_of
+                sent[layer, g, :, columns] = share_of.astype(bf16)
         for offset in range(1, groups):
             share(layer, offset).start()
 
-        for i in range(CHUNKS):
-            put_taps(i * size, incoming[i * size : (i + 1) * size, :])
-        for i in range(CHUNKS):
-            rows = slice(i * size, (i + 1) * size)
-            incoming[rows, :] += scaled[layer, rows, :] * conv(layer, i * size)
+        for i in range(PIECES):
+            put_taps(i * part, incoming[i * part : (i + 1) * part, :])
+        for i in range(PIECES):
+            rows = slice(i * part, (i + 1) * part)
+            incoming[rows, :] += scaled[layer, rows, :] * conv(layer, i * part, part)
 
     start_ref[...] = incoming[...].T
 
@@ -216,14 +251,14 @@
         total = parts[layer, member]
         for offset in range(1, groups):
             share(layer, offset).wait_recv()
-            total = total + landed[layer, offset - 1]
+            total = total + landed[layer, offset - 1].astype(f32)
         grads_ref[layer] = total
         for offset in range(1, groups):
             share(layer, offset).wait_send()
 
     @pl.when(position > 0)
     def _():
-        for i in range(CHUNKS):
+        for i in range(CHUNKS - FLYING, CHUNKS):
             hop(i).wait_send()
 
 
@@ -241,9 +276,13 @@
             jax.ShapeDtypeStruct((lanes, length), f32),
             jax.ShapeDtypeStruct((layers, rows, 9 * channels), f32),
         ),
-        in_specs=[pl.BlockSpec(memory_space=pltpu.VMEM)] * 4,
+        in_specs=[pl.BlockSpec(memory_space=pltpu.HBM)] * 4,
         out_specs=(pl.BlockSpec(memory_space=pltpu.VMEM),) * 2,
         scratch_shapes=[
+            pltpu.VMEM((layers, lanes, length), states.dtype),
+            pltpu.VMEM(weights.shape, weights.dtype),
+            pltpu.VMEM((lanes, length), f32),
+            pltpu.VMEM((lanes, length), f32),
             pltpu.VMEM((channels, 5 * lanes), f32),
             pltpu.VMEM((layers, 9 * lanes, lanes), bf16),
             pltpu.VMEM((layers, length, lanes), f32),
@@ -254,11 +293,13 @@
             pltpu.VMEM((length + 2 * side, 3 * lanes), bf16),
             pltpu.VMEM((layers, length + 2 * side, 3 * lanes), bf16),
             pltpu.VMEM((layers, groups, rows, 9 * channels), f32),
-            pltpu.VMEM((layers, groups - 1, rows, 9 * channels), f32),
+            pltpu.VMEM((layers, groups, rows, 9 * channels), bf16),
+            pltpu.VMEM((layers, groups - 1, rows, 9 * channels), bf16),
             pltpu.SemaphoreType.DMA((CHUNKS,)),
             pltpu.SemaphoreType.DMA((CHUNKS,)),
             pltpu.SemaphoreType.DMA((layers, groups - 1)),
             pltpu.SemaphoreType.DMA((layers, groups - 1)),
+            pltpu.SemaphoreType.DMA((4,)),
         ],
         compiler_params=pltpu.CompilerParams(
             collective_id=0, has_side_effects=True, vmem_limit_bytes=40 * 2**20

time: 49.1 us -> 44.1 us (0.90)
  Pallas kernels: 42.6 us -> 37.6 us
    pallas_call x1, Pallas kernels: 42.6 us -> 37.6 us  [shards(): pl.pallas_call(functools.partial(kernel, sections, groups, side), out_sha...]
where the time goes in v2:
time: 44.1 us; the launch traced here: 43.8 us
  Pallas kernels  37.6 us (85%)
  local copies, waits for them, and re-layouts  5.57 us (13%)
  between operations  0.65 us (1%)
    pallas_call x1, Pallas kernels, shards(): pl.pallas_call(functools.partial(kernel, sections, groups, side), out_sha...  37.6 us
    unnamed x9, local copies, waits for them, and re-layouts  4.82 us

profile of v2, /device:TPU:0, one launch (start us, length us, event | category | flops | bytes accessed | tf_op | source)
XLA Modules:
  0.0 43.8 jit_solution(2054865209471062499)
XLA Ops:
  0.6 0.0 copy-start
  0.6 1.0 %copy-done = bf16[2,2,64,1024]{3,2,1,0:T(8,128)(2,1)S(1)} copy-done((bf16[2,2,64,1024]{3,2,1,0:T(8,128)(2,1)S(1)}, bf16[2,2,64,1024]{3,2,1,0:T(8,128)(2,1)}, u32[]{:S(2)}) %copy-start) | copy-done | bytes 524312
  1.7 0.0 copy-start.1
  1.7 1.0 %copy-done.1 = f32[1,2,64,1024]{3,2,1,0:T(8,128)S(1)} copy-done((f32[1,2,64,1024]{3,2,1,0:T(8,128)S(1)}, f32[1,2,64,1024]{3,2,1,0:T(8,128)}, u32[]{:S(2)}) %copy-start.1) | copy-done | bytes 524312
  2.7 0.0 copy-start.2
  2.7 1.0 %copy-done.2 = f32[2,64,1024]{2,1,0:T(8,128)S(1)} copy-done((f32[2,64,1024]{2,1,0:T(8,128)S(1)}, f32[2,64,1024]{2,1,0:T(8,128)}, u32[]{:S(2)}) %copy-start.2) | copy-done | bytes 524312
  3.8 0.0 copy-start.3
  3.8 0.9 %copy-done.3 = bf16[2,64,576]{2,1,0:T(8,128)(2,1)S(1)} copy-done((bf16[2,64,576]{2,1,0:T(8,128)(2,1)S(1)}, bf16[2,64,576]{2,1,0:T(8,128)(2,1)}, u32[]{:S(2)}) %copy-start.3) | copy-done | bytes 147480
  4.7 37.6 %shard_map.59 = (f32[128,1024]{1,0:T(8,128)S(1)}, f32[2,16,576]{2,1,0:T(8,128)S(1)}) custom-call(bf16[2,128,1024]{2,1,0:T(8,128)(2,1)S(1)} %bitcast.4, bf16[2,64,576]{2,1,0:T(8,128)(2,1)S(1)} %copy-done.3, f32[128,1024]{1,0:T(8,128)S(1)} %bitcast.5, f32[128,1024]{1,0:T(8,128)S(1)} %bitcast.6), custom_call_target="tpu_custom_call" | custom-call | tf_op jit(solution)/shard_map/pallas_call | solution.py:273
  42.3 0.7 %reshape.23 = f32[2,9216]{1,0:T(2,128)} reshape(f32[2,16,576]{2,1,0:T(8,128)S(1)} %get-tuple-element.5) | data formatting | bytes 147456 | tf_op jit(solution)/shard_map/reshape | solution.py:313
  43.0 0.8 %copy.7 = f32[1,2,64,1024]{3,2,1,0:T(8,128)} copy(f32[1,2,64,1024]{3,2,1,0:T(8,128)S(1)} %bitcast.7) | data formatting | bytes 1048576
Async XLA Ops:
  0.6 1.0 %copy-start = (bf16[2,2,64,1024]{3,2,1,0:T(8,128)(2,1)S(1)}, bf16[2,2,64,1024]{3,2,1,0:T(8,128)(2,1)}, u32[]{:S(2)}) copy-start(bf16[2,2,64,1024]{3,2,1,0:T(8,128)(2,1)} %param.4) | copy-start | bytes 1572868
  1.7 1.0 %copy-start.1 = (f32[1,2,64,1024]{3,2,1,0:T(8,128)S(1)}, f32[1,2,64,1024]{3,2,1,0:T(8,128)}, u32[]{:S(2)}) copy-start(f32[1,2,64,1024]{3,2,1,0:T(8,128)} %param.6) | copy-start | bytes 1572868
  2.7 1.0 %copy-start.2 = (f32[2,64,1024]{2,1,0:T(8,128)S(1)}, f32[2,64,1024]{2,1,0:T(8,128)}, u32[]{:S(2)}) copy-start(f32[2,64,1024]{2,1,0:T(8,128)} %param.7) | copy-start | bytes 1572868
  3.8 0.9 %copy-start.3 = (bf16[2,64,576]{2,1,0:T(8,128)(2,1)S(1)}, bf16[2,64,576]{2,1,0:T(8,128)(2,1)}, u32[]{:S(2)}) copy-start(bf16[2,64,576]{2,1,0:T(8,128)(2,1)} %weights_hbm.1) | copy-start | bytes 442372

commit v3 on v2

--- a/solution.py
+++ b/solution.py
@@ -173,7 +173,9 @@
             + layers * scaled[0, rows, :] * conv(0, i * size, size)
         )
         if i >= FLYING:
-            hop(i - FLYING).wait_send()
+            @pl.when(position % 2 == 0)
+            def _():
+                hop(i - FLYING).wait_send()
         hop(i).start()
 
     for i in range(CHUNKS):
@@ -255,6 +257,11 @@
         grads_ref[layer] = total
         for offset in range(1, groups):
             share(layer, offset).wait_send()
+
+    @pl.when(position % 2 == 1)
+    def _():
+        for i in range(CHUNKS - FLYING):
+            hop(i).wait_send()
 
     @pl.when(position > 0)
     def _():
@@ -302,7 +309,7 @@
             pltpu.SemaphoreType.DMA((4,)),
         ],
         compiler_params=pltpu.CompilerParams(
-            collective_id=0, has_side_effects=True, vmem_limit_bytes=40 * 2**20
+            collective_id=0, has_side_effects=True, vmem_limit_bytes=63 * 2**20
         ),
     )(
         states.reshape(layers, lanes, length),

time: 44.1 us -> 43.5 us (0.986)
  local copies, waits for them, and re-layouts: 5.57 us -> 3.52 us
  Pallas kernels: 37.6 us -> 39.1 us
    unnamed x9 -> x1, local copies, waits for them, and re-layouts: 4.82 us -> 1.88 us
    pallas_call x1, Pallas kernels: 37.6 us -> 39.1 us  [shards(): pl.pallas_call(functools.partial(kernel, sections, groups, side), out_sha...]
    reshape x1, local copies, waits for them, and re-layouts: 0.75 us -> 1.63 us  [shards(): grads.reshape(layers, rows * 9 * channels)]
where the time goes in v3:
time: 43.5 us; the launch traced here: 43.2 us
  Pallas kernels  39.1 us (90%)
  local copies, waits for them, and re-layouts  3.52 us (8%)
  between operations  0.64 us (1%)
    pallas_call x1, Pallas kernels, shards(): pl.pallas_call(functools.partial(kernel, sections, groups, side), out_sha...  39.1 us
    unnamed x1, local copies, waits for them, and re-layouts  1.88 us
    reshape x1, local copies, waits for them, and re-layouts, shards(): grads.reshape(layers, rows * 9 * channels)  1.63 us

profile of v3, /device:TPU:0, one launch (start us, length us, event | category | flops | bytes accessed | tf_op | source)
XLA Modules:
  0.0 43.2 jit_solution(3102052619862444917)
XLA Ops:
  0.6 39.1 %shard_map.59 = (f32[128,1024]{1,0:T(8,128)}, f32[2,16,576]{2,1,0:T(8,128)}) custom-call(bf16[2,128,1024]{2,1,0:T(8,128)(2,1)} %bitcast.4, bf16[2,64,576]{2,1,0:T(8,128)(2,1)} %weights_hbm.1, f32[128,1024]{1,0:T(8,128)} %bitcast.5, f32[128,1024]{1,0:T(8,128)} %bitcast.6), custom_call_target="tpu_custom_call" | custom-call | tf_op jit(solution)/shard_map/pallas_call | solution.py:280
  39.7 1.6 %reshape.23 = f32[2,9216]{1,0:T(2,128)} reshape(f32[2,16,576]{2,1,0:T(8,128)} %get-tuple-element.5) | data formatting | bytes 147456 | tf_op jit(solution)/shard_map/reshape | solution.py:320
  41.3 1.9 %copy.7 = f32[1,2,64,1024]{3,2,1,0:T(8,128)} copy(f32[1,2,64,1024]{3,2,1,0:T(8,128)} %bitcast.7) | data formatting | bytes 1048576

commit v4 on v3

--- a/solution.py
+++ b/solution.py
@@ -19,8 +19,8 @@
     sections, groups, side,
     states_hbm, weights_hbm, guess_hbm, loss_hbm, start_ref, grads_ref,
     states_ref, weights_ref, guess_ref, loss_ref,
-    wide, blocks, scaled, held, base, incoming, outgoing, taps, acts, parts, sent, landed,
-    send_sem, recv_sem, part_send, part_recv, load_sem,
+    wide, blocks, scaled, held, base, incoming, left_over, high_in, high_out, low_in, low_out, taps, acts, parts, sent, landed,
+    send_sem, recv_sem, low_send, low_recv, part_send, part_recv, load_sem,
 ):
     position = lax.axis_index("section")
     member = lax.axis_index("batch")
@@ -135,6 +135,7 @@
     held[...] = guess_ref[...].T
 
     base[...] = jnp.zeros_like(base)
+    left_over[...] = jnp.zeros_like(left_over)
     for layer in range(layers - 1, -1, -1):
         for i in range(PIECES):
             rows = slice(i * part, (i + 1) * part)
@@ -155,23 +156,29 @@
     )
     pl.semaphore_wait(barrier, neighbours)
 
-    def hop(i):
+    def hop(i, source=high_out, target=high_in, sends=send_sem, receives=recv_sem):
         rows = pl.ds(i * size, size)
         return pltpu.make_async_remote_copy(
-            src_ref=outgoing.at[rows, :],
-            dst_ref=incoming.at[rows, :],
-            send_sem=send_sem.at[i],
-            recv_sem=recv_sem.at[i],
+            src_ref=source.at[rows, :],
+            dst_ref=target.at[rows, :],
+            send_sem=sends.at[i],
+            recv_sem=receives.at[i],
             device_id={"section": position - 1},
             device_id_type=MESH,
         )
 
+    def low_hop(i):
+        return hop(i, low_out, low_in, low_send, low_recv)
+
     def carry(i):
         rows = slice(i * size, (i + 1) * size)
-        outgoing[rows, :] = (
+        value = (
             incoming[rows, :] + base[rows, :]
             + layers * scaled[0, rows, :] * conv(0, i * size, size)
         )
+        high = value.astype(bf16)
+        high_out[rows, :] = high
+        left_over[rows, :] = value - high.astype(f32)
         if i >= FLYING:
             @pl.when(position % 2 == 0)
             def _():
@@ -181,7 +188,9 @@
     for i in range(CHUNKS):
         @pl.when(position < sections - 1)
         def _():
+            rows = slice(i * size, (i + 1) * size)
             hop(i).wait_recv()
+            incoming[rows, :] = high_in[rows, :].astype(f32)
 
         @pl.when(position > 0)
         def _():
@@ -193,6 +202,21 @@
     @pl.when(position > 0)
     def _():
         carry(CHUNKS - 1)
+
+    for i in range(CHUNKS):
+        @pl.when(position < sections - 1)
+        def _():
+            rows = slice(i * size, (i + 1) * size)
+            low_hop(i).wait_recv()
+            low_part = low_in[rows, :].astype(f32)
+            incoming[rows, :] += low_part
+            left_over[rows, :] += low_part
+
+        @pl.when(position > 0)
+        def _():
+            rows = slice(i * size, (i + 1) * size)
+            low_out[rows, :] = left_over[rows, :].astype(bf16)
+            low_hop(i).start()
 
     @pl.when(position == sections - 1)
     def _():
@@ -267,6 +291,8 @@
     def _():
         for i in range(CHUNKS - FLYING, CHUNKS):
             hop(i).wait_send()
+        for i in range(CHUNKS):
+            low_hop(i).wait_send()
 
 
 def shards(states, weights, guess, loss_cotangent):
@@ -297,11 +323,17 @@
             pltpu.VMEM((length, lanes), f32),
             pltpu.VMEM((length, lanes), f32),
             pltpu.VMEM((length, lanes), f32),
+            pltpu.VMEM((length, lanes), bf16),
+            pltpu.VMEM((length, lanes), bf16),
+            pltpu.VMEM((length, lanes), bf16),
+            pltpu.VMEM((length, lanes), bf16),
             pltpu.VMEM((length + 2 * side, 3 * lanes), bf16),
             pltpu.VMEM((layers, length + 2 * side, 3 * lanes), bf16),
             pltpu.VMEM((layers, groups, rows, 9 * channels), f32),
             pltpu.VMEM((layers, groups, rows, 9 * channels), bf16),
             pltpu.VMEM((layers, groups - 1, rows, 9 * channels), bf16),
+            pltpu.SemaphoreType.DMA((CHUNKS,)),
+            pltpu.SemaphoreType.DMA((CHUNKS,)),
             pltpu.SemaphoreType.DMA((CHUNKS,)),
             pltpu.SemaphoreType.DMA((CHUNKS,)),
             pltpu.SemaphoreType.DMA((layers, groups - 1)),

time: 43.5 us -> 42.9 us (0.986)
  Pallas kernels: 39.1 us -> 38.5 us
    pallas_call x1, Pallas kernels: 39.1 us -> 38.5 us  [shards(): pl.pallas_call(functools.partial(kernel, sections, groups, side), out_sha...]
where the time goes in v4:
time: 42.9 us; the launch traced here: 42.7 us
  Pallas kernels  38.5 us (90%)
  local copies, waits for them, and re-layouts  3.52 us (8%)
  between operations  0.64 us (1%)
    pallas_call x1, Pallas kernels, shards(): pl.pallas_call(functools.partial(kernel, sections, groups, side), out_sha...  38.5 us
    unnamed x1, local copies, waits for them, and re-layouts  1.88 us
    reshape x1, local copies, waits for them, and re-layouts, shards(): grads.reshape(layers, rows * 9 * channels)  1.63 us

profile of v4, /device:TPU:0, one launch (start us, length us, event | category | flops | bytes accessed | tf_op | source)
XLA Modules:
  0.0 42.7 jit_solution(5374848088017560380)
XLA Ops:
  0.6 38.5 %shard_map.59 = (f32[128,1024]{1,0:T(8,128)}, f32[2,16,576]{2,1,0:T(8,128)}) custom-call(bf16[2,128,1024]{2,1,0:T(8,128)(2,1)} %bitcast.4, bf16[2,64,576]{2,1,0:T(8,128)(2,1)} %weights_hbm.1, f32[128,1024]{1,0:T(8,128)} %bitcast.5, f32[128,1024]{1,0:T(8,128)} %bitcast.6), custom_call_target="tpu_custom_call" | custom-call | tf_op jit(solution)/shard_map/pallas_call | solution.py:306
  39.2 1.6 %reshape.23 = f32[2,9216]{1,0:T(2,128)} reshape(f32[2,16,576]{2,1,0:T(8,128)} %get-tuple-element.5) | data formatting | bytes 147456 | tf_op jit(solution)/shard_map/reshape | solution.py:352
  40.8 1.9 %copy.7 = f32[1,2,64,1024]{3,2,1,0:T(8,128)} copy(f32[1,2,64,1024]{3,2,1,0:T(8,128)} %bitcast.7) | data formatting | bytes 1048576

commit v5 on v4

--- a/solution.py
+++ b/solution.py
@@ -216,6 +216,10 @@
         def _():
             rows = slice(i * size, (i + 1) * size)
             low_out[rows, :] = left_over[rows, :].astype(bf16)
+            if i >= FLYING:
+                @pl.when(position % 2 == 0)
+                def _():
+                    low_hop(i - FLYING).wait_send()
             low_hop(i).start()
 
     @pl.when(position == sections - 1)
@@ -286,12 +290,12 @@
     def _():
         for i in range(CHUNKS - FLYING):
             hop(i).wait_send()
+            low_hop(i).wait_send()
 
     @pl.when(position > 0)
     def _():
         for i in range(CHUNKS - FLYING, CHUNKS):
             hop(i).wait_send()
-        for i in range(CHUNKS):
             low_hop(i).wait_send()
 
 

time: 42.9 us -> 45.6 us (1.063)
  Pallas kernels: 38.5 us -> 41.2 us
    pallas_call x1, Pallas kernels: 38.5 us -> 41.2 us  [shards(): pl.pallas_call(functools.partial(kernel, sections, groups, side), out_sha...]
where the time goes in v5:
time: 45.6 us; the launch traced here: 45.3 us
  Pallas kernels  41.2 us (90%)
  local copies, waits for them, and re-layouts  3.52 us (8%)
  between operations  0.64 us (1%)
    pallas_call x1, Pallas kernels, shards(): pl.pallas_call(functools.partial(kernel, sections, groups, side), out_sha...  41.2 us
    unnamed x1, local copies, waits for them, and re-layouts  1.88 us
    reshape x1, local copies, waits for them, and re-layouts, shards(): grads.reshape(layers, rows * 9 * channels)  1.63 us

profile of v5, /device:TPU:0, one launch (start us, length us, event | category | flops | bytes accessed | tf_op | source)
XLA Modules:
  0.0 45.3 jit_solution(10320411154432067657)
XLA Ops:
  0.6 41.2 %shard_map.59 = (f32[128,1024]{1,0:T(8,128)}, f32[2,16,576]{2,1,0:T(8,128)}) custom-call(bf16[2,128,1024]{2,1,0:T(8,128)(2,1)} %bitcast.4, bf16[2,64,576]{2,1,0:T(8,128)(2,1)} %weights_hbm.1, f32[128,1024]{1,0:T(8,128)} %bitcast.5, f32[128,1024]{1,0:T(8,128)} %bitcast.6), custom_call_target="tpu_custom_call" | custom-call | tf_op jit(solution)/shard_map/pallas_call | solution.py:310
  41.8 1.6 %reshape.23 = f32[2,9216]{1,0:T(2,128)} reshape(f32[2,16,576]{2,1,0:T(8,128)} %get-tuple-element.5) | data formatting | bytes 147456 | tf_op jit(solution)/shard_map/reshape | solution.py:356
  43.5 1.9 %copy.7 = f32[1,2,64,1024]{3,2,1,0:T(8,128)} copy(f32[1,2,64,1024]{3,2,1,0:T(8,128)} %bitcast.7) | data formatting | bytes 1048576
